TPU v7x, 128 devices: a whole 4x4x4 slice. The times are simulated.
128 devices in a mesh: section: 2 (over core), seq: 4 (over x), wa: 16 (over z, y).
Axes of the slice: x: 4, y: 4, z: 4, core: 2. Of those that a mesh axis runs over, the one named last changes fastest.
Arguments:
- tokens: bfloat16 [4, 1024, 1024], P(None, 'seq'), may hold values from -6 to 6
- cotangent: float32 [4, 1024, 1024], P(None, 'seq'), may hold values from -6 to 6
- in_weight: bfloat16 [2, 1024, 3, 1024], P('section', None, None, 'wa'), may hold values from -0.1875 to 0.1875
- conv_weight: float32 [2, 3, 1024], P('section', None, 'wa'), may hold values from -3 to 3
- out_weight: bfloat16 [2, 1024, 1024], P('section', 'wa'), may hold values from -0.1875 to 0.1875
- norm_gain: float32 [2, 1024], P('section'), may hold values from 0.25 to 1.75
- gate_up_weight: bfloat16 [2, 1024, 2, 4608], P('section', None, None, 'wa'), may hold values from -0.1875 to 0.1875
- down_weight: bfloat16 [2, 4608, 1024], P('section', 'wa'), may hold values from -0.09375 to 0.09375
Outputs:
- layer_out: bfloat16 [2, 4, 1024, 1024], P('section', None, ('seq', 'wa'))
- input_grad: float32 [2, 4, 1024, 1024], P('section', None, ('seq', 'wa'))
- in_weight_grad: float32 [2, 1024, 3, 1024], P('section', None, None, 'wa')
- conv_weight_grad: float32 [2, 3, 1024], P('section', None, 'wa')
- out_weight_grad: float32 [2, 1024, 1024], P('section', 'wa')
- norm_gain_grad: float32 [2, 1024], P('section')
- gate_up_grad: float32 [2, 1024, 2, 4608], P('section', None, None, 'wa')
- down_grad: float32 [2, 4608, 1024], P('section', 'wa')
All inputs are finite; a program needn't handle non-finite values.
Results may differ from a plain program's by a relative error of at most 0.025.
Values may be sent and summed in bfloat16 or wider, within the bound.
A program may use at most 128 MiB of HBM per device.

v0:
```python
import jax
import jax.numpy as jnp
from jax import lax
from jax.sharding import PartitionSpec as P

EPSILON = 1e-05


def passed_along(block, axis, distance):
    devices = range(lax.axis_size(axis))
    route = [((i - distance) % len(devices), i) for i in devices]
    return lax.ppermute(block, axis, route)


def shifted(block, axis, distance):
    devices = range(lax.axis_size(axis))
    route = [(i - distance, i) for i in devices if i - distance in devices]
    return lax.ppermute(block, axis, route)


def contract_first(lhs_matrix, rhs_matrix):
    return lax.dot_general(
        lhs_matrix, rhs_matrix, (((0,), (0,)), ((), ())), preferred_element_type=jnp.float32
    )


def contract_last(lhs_matrix, rhs_matrix):
    return lax.dot_general(
        lhs_matrix, rhs_matrix, (((1,), (1,)), ((), ())), preferred_element_type=jnp.float32
    )


def silu_parts(gate_val):
    sigmoid_val = jax.nn.sigmoid(gate_val)
    return (gate_val * sigmoid_val, sigmoid_val * (1.0 + gate_val * (1.0 - sigmoid_val)))


def body(
    tokens, cotangent, in_weight, conv_weight, out_weight, norm_gain, gate_up_weight, down_weight
):
    micro_count, block_rows, model_width = tokens.shape
    section_index = lax.axis_index("section")
    seq_index = lax.axis_index("seq")
    seq_count = lax.axis_size("seq")
    wa_index = lax.axis_index("wa")
    share_rows = block_rows // lax.axis_size("wa")
    share_start = wa_index * share_rows
    local_width = conv_weight.shape[2]
    hidden_width = gate_up_weight.shape[3]
    in_matrix = in_weight[0].reshape(model_width, 3 * local_width)
    conv_taps = conv_weight[0]
    out_matrix = out_weight[0]
    gain_row = norm_gain[0]
    gate_up = gate_up_weight[0].reshape(model_width, 2 * hidden_width)
    down_matrix = down_weight[0]
    edge_zeros = jnp.zeros((2, local_width), jnp.bfloat16)
    received = jnp.zeros((block_rows, model_width), jnp.bfloat16)
    carried = edge_zeros
    outputs = []
    saved = []
    for step_num in range(micro_count + 1):
        micro_index = step_num - section_index
        inputs = jnp.where(section_index == 0, tokens[min(step_num, micro_count - 1)], received)
        projected = jnp.dot(inputs, in_matrix, preferred_element_type=jnp.float32).reshape(
            block_rows, 3, local_width
        )
        gated_in = (projected[:, 0] * projected[:, 2]).astype(jnp.bfloat16)
        incoming = passed_along(gated_in[block_rows - 2 :], "seq", 1)
        first_rows = jnp.where(
            seq_index == 0, jnp.where(micro_index == 0, edge_zeros, carried), incoming
        )
        carried = incoming
        padded = jnp.concatenate([first_rows, gated_in], 0).astype(jnp.float32)
        conv_out = (
            conv_taps[0] * padded[:block_rows]
            + conv_taps[1] * padded[1 : block_rows + 1]
            + conv_taps[2] * padded[2:]
        )
        mixed_in = (projected[:, 1] * conv_out).astype(jnp.bfloat16)
        mixed_sum = lax.psum(
            jnp.dot(mixed_in, out_matrix, preferred_element_type=jnp.float32), "wa"
        )
        residual = inputs.astype(jnp.float32) + mixed_sum
        inv_rms = lax.rsqrt(jnp.mean(residual * residual, -1, keepdims=True) + EPSILON)
        normed = (residual * inv_rms * gain_row).astype(jnp.bfloat16)
        gate_up_val = jnp.dot(normed, gate_up, preferred_element_type=jnp.float32).reshape(
            block_rows, 2, hidden_width
        )
        gate_val = gate_up_val[:, 0]
        up_val = gate_up_val[:, 1]
        hidden = (silu_parts(gate_val)[0] * up_val).astype(jnp.bfloat16)
        own_residual = lax.dynamic_slice_in_dim(residual, share_start, share_rows, 0)
        layer_rows = (
            own_residual
            + lax.psum_scatter(
                jnp.dot(hidden, down_matrix, preferred_element_type=jnp.float32),
                "wa",
                scatter_dimension=0,
                tiled=True,
            )
        ).astype(jnp.bfloat16)
        outputs.append(layer_rows)
        saved.append(
            (
                inputs,
                projected,
                padded,
                conv_out,
                mixed_in,
                residual,
                inv_rms,
                normed,
                gate_val,
                up_val,
                hidden,
            )
        )
        if step_num < micro_count:
            arrived = shifted(layer_rows, "section", 1)
            received = lax.all_gather(arrived, "wa", axis=0, tiled=True)
    stacked_out = jnp.stack(outputs)
    layer_block = jnp.where(section_index == 0, stacked_out[:micro_count], stacked_out[1:])
    tail_zeros = jnp.zeros((2, local_width), jnp.float32)
    received_grad = jnp.zeros((block_rows, model_width), jnp.float32)
    carried_grad = tail_zeros
    in_total = jnp.zeros((model_width, 3 * local_width), jnp.float32)
    tap_total = jnp.zeros((3, local_width), jnp.float32)
    out_total = jnp.zeros((local_width, model_width), jnp.float32)
    gain_total = jnp.zeros((model_width,), jnp.float32)
    gate_up_total = jnp.zeros((model_width, 2 * hidden_width), jnp.float32)
    down_total = jnp.zeros((hidden_width, model_width), jnp.float32)
    grad_rows = []
    for step_num in range(micro_count + 1):
        micro_index = micro_count - 1 - step_num + (1 - section_index)
        valid = (micro_index >= 0) & (micro_index < micro_count)
        (
            inputs,
            projected,
            padded,
            conv_out,
            mixed_in,
            residual,
            inv_rms,
            normed,
            gate_val,
            up_val,
            hidden,
        ) = saved[micro_count - step_num]
        out_grad = jnp.where(
            section_index == 1, cotangent[max(micro_count - 1 - step_num, 0)], received_grad
        )
        out_bf = out_grad.astype(jnp.bfloat16)
        hidden_grad = contract_last(out_bf, down_matrix)
        silu_val, silu_slope = silu_parts(gate_val)
        gate_up_bf = (
            jnp.stack([hidden_grad * up_val * silu_slope, hidden_grad * silu_val], 1)
            .astype(jnp.bfloat16)
            .reshape(block_rows, 2 * hidden_width)
        )
        normed_grad = lax.psum(
            contract_last(gate_up_bf, gate_up).astype(jnp.bfloat16), "wa"
        ).astype(jnp.float32)
        scaled_grad = normed_grad * gain_row
        gain_term = jnp.sum(normed_grad * residual * inv_rms, 0)
        residual_grad = (
            out_grad
            + inv_rms * scaled_grad
            - residual * inv_rms**3 * jnp.mean(scaled_grad * residual, -1, keepdims=True)
        )
        residual_bf = residual_grad.astype(jnp.bfloat16)
        mixed_grad = contract_last(residual_bf, out_matrix)
        c_grad = mixed_grad * conv_out
        conv_grad = mixed_grad * projected[:, 1]
        incoming_grad = passed_along(conv_grad[:2], "seq", -1)
        last_rows = jnp.where(
            seq_index == seq_count - 1,
            jnp.where(micro_index == micro_count - 1, tail_zeros, carried_grad),
            incoming_grad,
        )
        carried_grad = incoming_grad
        extended = jnp.concatenate([conv_grad, last_rows], 0)
        gated_grad = (
            conv_taps[2] * extended[:block_rows]
            + conv_taps[1] * extended[1 : block_rows + 1]
            + conv_taps[0] * extended[2:]
        )
        tap_grad = jnp.stack(
            [jnp.sum(conv_grad * padded[offset : offset + block_rows], 0) for offset in range(3)]
        )
        proj_bf = (
            jnp.stack([gated_grad * projected[:, 2], c_grad, gated_grad * projected[:, 0]], 1)
            .astype(jnp.bfloat16)
            .reshape(block_rows, 3 * local_width)
        )
        own_grad = lax.dynamic_slice_in_dim(residual_grad, share_start, share_rows, 0)
        input_rows_grad = own_grad + lax.psum_scatter(
            contract_last(proj_bf, in_matrix).astype(jnp.bfloat16),
            "wa",
            scatter_dimension=0,
            tiled=True,
        ).astype(jnp.float32)
        grad_rows.append(input_rows_grad)
        in_total = in_total + jnp.where(valid, contract_first(inputs, proj_bf), 0.0)
        tap_total = tap_total + jnp.where(valid, tap_grad, 0.0)
        out_total = out_total + jnp.where(valid, contract_first(mixed_in, residual_bf), 0.0)
        gain_total = gain_total + jnp.where(valid, gain_term, 0.0)
        gate_up_total = gate_up_total + jnp.where(valid, contract_first(normed, gate_up_bf), 0.0)
        down_total = down_total + jnp.where(valid, contract_first(hidden, out_bf), 0.0)
        if step_num < micro_count:
            arrived_grad = shifted(input_rows_grad.astype(jnp.bfloat16), "section", -1).astype(
                input_rows_grad.dtype
            )
            received_grad = lax.all_gather(
                arrived_grad.astype(jnp.bfloat16), "wa", axis=0, tiled=True
            ).astype(arrived_grad.dtype)
    stacked_grad = jnp.stack(grad_rows)
    grad_block = jnp.where(section_index == 1, stacked_grad[:micro_count], stacked_grad[1:])[::-1]
    in_sum, tap_sum, out_sum, gain_sum, gate_up_sum, down_sum = (
        lax.psum(in_total.astype(jnp.bfloat16), "seq").astype(jnp.float32),
        lax.psum(tap_total.astype(jnp.bfloat16), "seq").astype(jnp.float32),
        lax.psum(out_total.astype(jnp.bfloat16), "seq").astype(jnp.float32),
        lax.psum(gain_total.astype(jnp.bfloat16), "seq").astype(jnp.float32),
        lax.psum(gate_up_total.astype(jnp.bfloat16), "seq").astype(jnp.float32),
        lax.psum(down_total.astype(jnp.bfloat16), "seq").astype(jnp.float32),
    )
    return (
        layer_block[None],
        grad_block[None],
        in_sum.reshape(1, model_width, 3, local_width),
        tap_sum[None],
        out_sum[None],
        gain_sum[None],
        gate_up_sum.reshape(1, model_width, 2, hidden_width),
        down_sum[None],
    )


def solution(mesh):
    in_specs = (
        P(None, "seq", None),
        P(None, "seq", None),
        P("section", None, None, "wa"),
        P("section", None, "wa"),
        P("section", "wa", None),
        P("section", None),
        P("section", None, None, "wa"),
        P("section", "wa", None),
    )
    out_specs = (
        P("section", None, ("seq", "wa"), None),
        P("section", None, ("seq", "wa"), None),
        P("section", None, None, "wa"),
        P("section", None, "wa"),
        P("section", "wa", None),
        P("section", None),
        P("section", None, None, "wa"),
        P("section", "wa", None),
    )
    return jax.shard_map(body, mesh=mesh, in_specs=in_specs, out_specs=out_specs, check_vma=False)
```

profile of v0, /device:TPU:1, one launch (start us, length us, event | category | flops | bytes accessed | tf_op | source)
XLA Modules:
  0.0 2037.2 jit_solution(783066171614633669)
XLA Ops:
  16.3 88.3 %all-reduce.14.cloned.1.call-done = f32[256,1024]{1,0:T(8,128)} async-done(((f32[256,1024]{1,0:T(8,128)}), f32[256,1024]{1,0:T(8,128)}) %all-reduce.14.cloned.1.call-update) | async-done | bytes 1048592 | tf_op jit(solution)/shard_map/psum | solution.py:80
  109.4 72.1 %reduce-scatter.11.cloned.1.call-done = f32[16,1024]{1,0:T(8,128)} async-done(((f32[256,1024]{1,0:T(8,128)}), f32[16,1024]{1,0:T(8,128)}) %reduce-scatter.11.cloned.1.call-update) | async-done | bytes 65552 | tf_op jit(solution)/shard_map/reduce_scatter | solution.py:95
  186.6 18.4 all_gather.24
  213.2 88.8 %all-reduce.16.cloned.1.call-done = f32[256,1024]{1,0:T(8,128)} async-done(((f32[256,1024]{1,0:T(8,128)}), f32[256,1024]{1,0:T(8,128)}) %all-reduce.16.cloned.1.call-update) | async-done | bytes 1048592 | tf_op jit(solution)/shard_map/psum | solution.py:80
  307.0 72.1 %reduce-scatter.13.cloned.1.call-done = f32[16,1024]{1,0:T(8,128)} async-done(((f32[256,1024]{1,0:T(8,128)}), f32[16,1024]{1,0:T(8,128)}) %reduce-scatter.13.cloned.1.call-update) | async-done | bytes 65552 | tf_op jit(solution)/shard_map/reduce_scatter | solution.py:95
  384.2 18.4 all_gather.25
  416.7 88.8 %all-reduce.18.cloned.1.call-done = f32[256,1024]{1,0:T(8,128)} async-done(((f32[256,1024]{1,0:T(8,128)}), f32[256,1024]{1,0:T(8,128)}) %all-reduce.18.cloned.1.call-update) | async-done | bytes 1048592 | tf_op jit(solution)/shard_map/psum | solution.py:80
  510.7 72.1 %reduce-scatter.15.cloned.1.call-done = f32[16,1024]{1,0:T(8,128)} async-done(((f32[256,1024]{1,0:T(8,128)}), f32[16,1024]{1,0:T(8,128)}) %reduce-scatter.15.cloned.1.call-update) | async-done | bytes 65552 | tf_op jit(solution)/shard_map/reduce_scatter | solution.py:95
  588.0 18.4 all_gather.26
  620.5 88.8 %all-reduce.20.cloned.1.call-done = f32[256,1024]{1,0:T(8,128)} async-done(((f32[256,1024]{1,0:T(8,128)}), f32[256,1024]{1,0:T(8,128)}) %all-reduce.20.cloned.1.call-update) | async-done | bytes 1048592 | tf_op jit(solution)/shard_map/psum | solution.py:80
  714.5 72.2 %reduce-scatter.17.cloned.1.call-done = f32[16,1024]{1,0:T(8,128)} async-done(((f32[256,1024]{1,0:T(8,128)}), f32[16,1024]{1,0:T(8,128)}) %reduce-scatter.17.cloned.1.call-update) | async-done | bytes 65552 | tf_op jit(solution)/shard_map/reduce_scatter | solution.py:95
  791.8 18.4 all_gather.27
  824.5 88.7 %all-reduce.22.cloned.1.call-done = f32[256,1024]{1,0:T(8,128)} async-done(((f32[256,1024]{1,0:T(8,128)}), f32[256,1024]{1,0:T(8,128)}) %all-reduce.22.cloned.1.call-update) | async-done | bytes 1048592 | tf_op jit(solution)/shard_map/psum | solution.py:80
  921.0 84.7 %all-reduce.24.cloned.1.call-done = bf16[256,1024]{1,0:T(8,128)(2,1)} async-done(((bf16[256,1024]{1,0:T(8,128)(2,1)}), bf16[256,1024]{1,0:T(8,128)(2,1)}) %all-reduce.24.cloned.1.call-update) | async-done | bytes 524304 | tf_op jit(solution)/shard_map/psum | solution.py:160
  1016.2 72.9 %reduce-scatter.21.cloned.1.call-done = bf16[16,1024]{1,0:T(8,128)(2,1)} async-done(((bf16[256,1024]{1,0:T(8,128)(2,1)}), bf16[16,1024]{1,0:T(8,128)(2,1)}) %reduce-scatter.21.cloned.1.call-update) | async-done | bytes 32784 | tf_op jit(solution)/shard_map/reduce_scatter | solution.py:196
  1095.7 18.2 all_gather.28
  1118.2 87.4 %all-reduce.26.cloned.1.call-done = bf16[256,1024]{1,0:T(8,128)(2,1)} async-done(((bf16[256,1024]{1,0:T(8,128)(2,1)}), bf16[256,1024]{1,0:T(8,128)(2,1)}) %all-reduce.26.cloned.1.call-update) | async-done | bytes 524304 | tf_op jit(solution)/shard_map/psum | solution.py:160
  1216.4 72.9 %reduce-scatter.23.cloned.1.call-done = bf16[16,1024]{1,0:T(8,128)(2,1)} async-done(((bf16[256,1024]{1,0:T(8,128)(2,1)}), bf16[16,1024]{1,0:T(8,128)(2,1)}) %reduce-scatter.23.cloned.1.call-update) | async-done | bytes 32784 | tf_op jit(solution)/shard_map/reduce_scatter | solution.py:196
  1295.8 18.2 all_gather.29
  1318.4 87.5 %all-reduce.28.cloned.1.call-done = bf16[256,1024]{1,0:T(8,128)(2,1)} async-done(((bf16[256,1024]{1,0:T(8,128)(2,1)}), bf16[256,1024]{1,0:T(8,128)(2,1)}) %all-reduce.28.cloned.1.call-update) | async-done | bytes 524304 | tf_op jit(solution)/shard_map/psum | solution.py:160
  1416.5 72.9 %reduce-scatter.25.cloned.1.call-done = bf16[16,1024]{1,0:T(8,128)(2,1)} async-done(((bf16[256,1024]{1,0:T(8,128)(2,1)}), bf16[16,1024]{1,0:T(8,128)(2,1)}) %reduce-scatter.25.cloned.1.call-update) | async-done | bytes 32784 | tf_op jit(solution)/shard_map/reduce_scatter | solution.py:196
  1495.9 18.1 all_gather.30
  1518.6 87.3 %all-reduce.30.cloned.1.call-done = bf16[256,1024]{1,0:T(8,128)(2,1)} async-done(((bf16[256,1024]{1,0:T(8,128)(2,1)}), bf16[256,1024]{1,0:T(8,128)(2,1)}) %all-reduce.30.cloned.1.call-update) | async-done | bytes 524304 | tf_op jit(solution)/shard_map/psum | solution.py:160
  1617.3 71.7 %reduce-scatter.27.cloned.1.call-done = bf16[16,1024]{1,0:T(8,128)(2,1)} async-done(((bf16[256,1024]{1,0:T(8,128)(2,1)}), bf16[16,1024]{1,0:T(8,128)(2,1)}) %reduce-scatter.27.cloned.1.call-update) | async-done | bytes 32784 | tf_op jit(solution)/shard_map/reduce_scatter | solution.py:196
  1690.5 4.3 collective-permute-start.16
  1697.4 18.6 all_gather.31
  1743.4 63.0 %all-reduce.32.cloned.1.call-done = bf16[256,1024]{1,0:T(8,128)(2,1)} async-done(((bf16[256,1024]{1,0:T(8,128)(2,1)}), bf16[256,1024]{1,0:T(8,128)(2,1)}) %all-reduce.32.cloned.1.call-update) | async-done | bytes 524304 | tf_op jit(solution)/shard_map/psum | solution.py:160
  1816.5 5.9 add_convert_fusion
  1828.8 53.3 %reduce-scatter.19.cloned.1.call-done = f32[16,1024]{1,0:T(8,128)} async-done(((f32[256,1024]{1,0:T(8,128)}), f32[16,1024]{1,0:T(8,128)}) %reduce-scatter.19.cloned.1.call-update) | async-done | bytes 65552 | tf_op jit(solution)/shard_map/reduce_scatter | solution.py:95
  1883.9 8.5 all-reduce
  1893.6 63.2 %reduce-scatter.29.cloned.1.call-done = bf16[16,1024]{1,0:T(8,128)(2,1)} async-done(((bf16[256,1024]{1,0:T(8,128)(2,1)}), bf16[16,1024]{1,0:T(8,128)(2,1)}) %reduce-scatter.29.cloned.1.call-update) | async-done | bytes 32784 | tf_op jit(solution)/shard_map/reduce_scatter | solution.py:196
  1958.3 65.0 %all-reduce.34.cloned.1.call-done = (bf16[1,1024,3,64]{1,3,2,0:T(8,128)(2,1)}, bf16[1,64,1024]{2,1,0:T(8,128)(2,1)}, bf16[1,1024,2,288]{1,3,2,0:T(8,128)(2,1)}, bf16[1,288,1024]{2,1,0:T(8,128)(2,1)}) async-done(((bf16[1,1024,3,64]{1,3,2,0:T(8,128)(2,1)}, bf16[1,64,1024]{2,1,0:T(8,128)(2,1)}, bf16[1,1024,2,288]{1,3,2,0:T(8,128)(2,1)}, bf16[1,288,1024]{2,1,0:T(8,128)(2,1)}), ...) | async-done | bytes 2293776 | tf_op jit(solution)/shard_map/psum | solution.py:219
  (594 shorter events, 241.7 us)
Async XLA Ops:
  7.2 97.4 %all-reduce.14.cloned.1.call-start = ((), (), s32[]{:S(2)}) async-start(), calls=%async_computation.10 | async-start | bytes 2097152 | tf_op jit(solution)/shard_map/psum | solution.py:80
  8.9 4.4 collective-permute-start
  16.2 165.3 %reduce-scatter.11.cloned.1.call-start = ((), (), s32[]{:S(2)}) async-start(), calls=%async_computation.11 | async-start | bytes 1114112 | tf_op jit(solution)/shard_map/reduce_scatter | solution.py:95
  109.4 192.6 %all-reduce.16.cloned.1.call-start = ((), (), s32[]{:S(2)}) async-start(), calls=%async_computation.12 | async-start | bytes 2097152 | tf_op jit(solution)/shard_map/psum | solution.py:80
  182.4 4.2 collective-permute-start.1
  213.1 166.0 %reduce-scatter.13.cloned.1.call-start = ((), (), s32[]{:S(2)}) async-start(), calls=%async_computation.13 | async-start | bytes 1114112 | tf_op jit(solution)/shard_map/reduce_scatter | solution.py:95
  307.0 198.6 %all-reduce.18.cloned.1.call-start = ((), (), s32[]{:S(2)}) async-start(), calls=%async_computation.14 | async-start | bytes 2097152 | tf_op jit(solution)/shard_map/psum | solution.py:80
  380.0 4.3 collective-permute-start.3
  406.9 4.1 collective-permute-start.4
  416.7 166.2 %reduce-scatter.15.cloned.1.call-start = ((), (), s32[]{:S(2)}) async-start(), calls=%async_computation.15 | async-start | bytes 1114112 | tf_op jit(solution)/shard_map/reduce_scatter | solution.py:95
  510.7 198.6 %all-reduce.20.cloned.1.call-start = ((), (), s32[]{:S(2)}) async-start(), calls=%async_computation.16 | async-start | bytes 2097152 | tf_op jit(solution)/shard_map/psum | solution.py:80
  583.8 4.2 collective-permute-start.5
  610.6 4.1 collective-permute-start.6
  620.4 166.3 %reduce-scatter.17.cloned.1.call-start = ((), (), s32[]{:S(2)}) async-start(), calls=%async_computation.17 | async-start | bytes 1114112 | tf_op jit(solution)/shard_map/reduce_scatter | solution.py:95
  714.5 198.7 %all-reduce.22.cloned.1.call-start = ((), (), s32[]{:S(2)}) async-start(), calls=%async_computation.18 | async-start | bytes 2097152 | tf_op jit(solution)/shard_map/psum | solution.py:80
  787.6 4.2 collective-permute-start.7
  824.2 181.5 %all-reduce.24.cloned.1.call-start = ((), (), s32[]{:S(2)}) async-start(), calls=%async_computation.20 | async-start | bytes 1048576 | tf_op jit(solution)/shard_map/psum | solution.py:160
  921.0 168.2 %reduce-scatter.21.cloned.1.call-start = ((), (), s32[]{:S(2)}) async-start(), calls=%async_computation.21 | async-start | bytes 557056 | tf_op jit(solution)/shard_map/reduce_scatter | solution.py:196
  1016.2 189.4 %all-reduce.26.cloned.1.call-start = ((), (), s32[]{:S(2)}) async-start(), calls=%async_computation.22 | async-start | bytes 1048576 | tf_op jit(solution)/shard_map/psum | solution.py:160
  1090.7 5.0 collective-permute-start.10
  1118.1 171.2 %reduce-scatter.23.cloned.1.call-start = ((), (), s32[]{:S(2)}) async-start(), calls=%async_computation.23 | async-start | bytes 557056 | tf_op jit(solution)/shard_map/reduce_scatter | solution.py:196
  1216.3 189.5 %all-reduce.28.cloned.1.call-start = ((), (), s32[]{:S(2)}) async-start(), calls=%async_computation.24 | async-start | bytes 1048576 | tf_op jit(solution)/shard_map/psum | solution.py:160
  1290.8 5.0 collective-permute-start.12
  1318.3 171.1 %reduce-scatter.25.cloned.1.call-start = ((), (), s32[]{:S(2)}) async-start(), calls=%async_computation.25 | async-start | bytes 557056 | tf_op jit(solution)/shard_map/reduce_scatter | solution.py:196
  1416.5 189.4 %all-reduce.30.cloned.1.call-start = ((), (), s32[]{:S(2)}) async-start(), calls=%async_computation.26 | async-start | bytes 1048576 | tf_op jit(solution)/shard_map/psum | solution.py:160
  1490.9 5.0 collective-permute-start.14
  1518.4 170.7 %reduce-scatter.27.cloned.1.call-start = ((), (), s32[]{:S(2)}) async-start(), calls=%async_computation.27 | async-start | bytes 557056 | tf_op jit(solution)/shard_map/reduce_scatter | solution.py:196
  1616.0 190.4 %all-reduce.32.cloned.1.call-start = ((), (), s32[]{:S(2)}) async-start(), calls=%async_computation.28 | async-start | bytes 1048576 | tf_op jit(solution)/shard_map/psum | solution.py:160
  1690.5 6.9 collective-permute-start.16
  1720.0 162.1 %reduce-scatter.19.cloned.1.call-start = ((), (), s32[]{:S(2)}) async-start(), calls=%async_computation.19 | async-start | bytes 1114112 | tf_op jit(solution)/shard_map/reduce_scatter | solution.py:95
  1725.9 230.9 %reduce-scatter.29.cloned.1.call-start = ((), (), s32[]{:S(2)}) async-start(), calls=%async_computation.29 | async-start | bytes 557056 | tf_op jit(solution)/shard_map/reduce_scatter | solution.py:196
  1816.2 207.2 %all-reduce.34.cloned.1.call-start = ((), (), s32[]{:S(2)}) async-start(), calls=%async_computation.30 | async-start | bytes 4587520 | tf_op jit(solution)/shard_map/psum | solution.py:219
  (180 other events, 2752.4 us)
Sparse Core Ops, SparseCore 0:
  16.3 88.1 all-reduce.13
  109.5 72.0 reduce-scatter.10
  213.3 88.7 all-reduce.15
  307.1 71.9 reduce-scatter.12
  416.8 88.6 all-reduce.17
  510.8 72.0 reduce-scatter.14
  620.6 88.7 all-reduce.19
  714.6 72.0 reduce-scatter.16
  824.3 88.7 all-reduce.21
  921.1 84.5 all-reduce.23
  1016.3 72.8 reduce-scatter.20
  1118.3 87.3 all-reduce.25
  1216.4 72.8 reduce-scatter.22
  1318.4 87.3 all-reduce.27
  1416.6 72.8 reduce-scatter.24
  1518.5 87.3 all-reduce.29
  1616.2 72.8 reduce-scatter.26
  1720.1 86.2 all-reduce.31
  1809.9 72.0 reduce-scatter.18
  1885.1 71.6 reduce-scatter.28
  1960.1 63.1 all-reduce.33
where the time goes:
time: 2040 us
  waiting for transfers between devices  1650 us (81%)
  blocking collectives  155 us (8%)
  matrix products  81.4 us (4%)
  other arithmetic  67.3 us (3%)
  starting transfers between devices  42.4 us (2%)
  local copies, waits for them, and re-layouts  28.3 us (1%)
    psum x5, waiting for transfers between devices, body(): lax.psum(jnp.dot(mixed_in, out_matrix, preferred_element_type=jnp.float32...  443 us
    psum x5, waiting for transfers between devices, body(): lax.psum(contract_last(gate_up_bf, gate_up).astype(jnp.bfloat16), 'wa')  410 us
    reduce_scatter x5, waiting for transfers between devices, body(): lax.psum_scatter(contract_last(proj_bf, in_matrix).astype(jnp.bfloat16),...  354 us
    reduce_scatter x5, waiting for transfers between devices, body(): lax.psum_scatter(jnp.dot(hidden, down_matrix, preferred_element_type=jnp....  342 us
    all_gather x4, blocking collectives, body(): received = lax.all_gather(arrived, 'wa', axis=0, tiled=True)  73.5 us
    all_gather x4, blocking collectives, body(): lax.all_gather(arrived_grad.astype(jnp.bfloat16), 'wa', axis=0, tiled=True)  73.1 us
    psum x1, waiting for transfers between devices, body(): lax.psum(in_total.astype(jnp.bfloat16), 'seq').astype(jnp.float32)  65 us
  transfers between devices with their start and end apart: 39, of which 37 were waited for; matrix products, arithmetic and copies ran while one was open for 2% of the time, Pallas kernels for 0%

commit v1 on v0

--- a/solution.py
+++ b/solution.py
@@ -4,6 +4,23 @@
 from jax.sharding import PartitionSpec as P
 
 EPSILON = 1e-05
+
+
+def _set_frames(own_rows, net_axis, along_dim):
+    many = lax.axis_size(net_axis)
+    field_out = range(1, many)
+    m_next = map(lambda pp: (pp - 1, pp), field_out)
+    high = list(m_next)
+    x_new = own_rows
+    fresh = high + [(many - 1, 0)]
+    rack = [x_new]
+    for _ in range(many - 1):
+        x_new = lax.ppermute(x_new, net_axis, fresh)
+        rack += [x_new]
+    local_part = jnp.concatenate([*reversed(rack)], axis=along_dim)
+    inter = lax.axis_index(net_axis)
+    t_next = jnp.roll(local_part, shift=(inter + 1) * x_new.shape[along_dim], axis=along_dim)
+    return t_next
 
 
 def passed_along(block, axis, distance):
@@ -117,7 +134,7 @@
         )
         if step_num < micro_count:
             arrived = shifted(layer_rows, "section", 1)
-            received = lax.all_gather(arrived, "wa", axis=0, tiled=True)
+            received = _set_frames(arrived, "wa", 0)
     stacked_out = jnp.stack(outputs)
     layer_block = jnp.where(section_index == 0, stacked_out[:micro_count], stacked_out[1:])
     tail_zeros = jnp.zeros((2, local_width), jnp.float32)

time: 2040 us -> 2380 us (1.17)
  waiting for transfers between devices: 1650 us -> 2050 us
  blocking collectives: 155 us -> 81.6 us
    ppermute x0 -> x60, waiting for transfers between devices: none -> 363 us  [_set_frames(): x_new = lax.ppermute(x_new, net_axis, fresh)]
    all_gather x4 -> x0, blocking collectives: 73.5 us -> none  [body(): received = lax.all_gather(arrived, 'wa', axis=0, tiled=True)]
    psum x5, waiting for transfers between devices: 443 us -> 481 us  [body(): lax.psum(jnp.dot(mixed_in, out_matrix, preferred_element_type=jnp.float32...]
  transfers between devices with their start and end apart: 39 -> 99, of which waited for: 37 -> 97; matrix products, arithmetic and copies ran while one was open for 2% -> 2% of each run, Pallas kernels for 0% -> 0%
where the time goes in v1:
time: 2380 us; the launch traced here: 2370 us
  waiting for transfers between devices  2050 us (86%)
  blocking collectives  81.6 us (3%)
  matrix products  81.5 us (3%)
  other arithmetic  69.5 us (3%)
  starting transfers between devices  46.9 us (2%)
  local copies, waits for them, and re-layouts  28.7 us (1%)
    psum x5, waiting for transfers between devices, body(): lax.psum(jnp.dot(mixed_in, out_matrix, preferred_element_type=jnp.float32...  481 us
    psum x5, waiting for transfers between devices, body(): lax.psum(contract_last(gate_up_bf, gate_up).astype(jnp.bfloat16), 'wa')  410 us
    ppermute x60, waiting for transfers between devices, _set_frames(): x_new = lax.ppermute(x_new, net_axis, fresh)  363 us
    reduce_scatter x5, waiting for transfers between devices, body(): lax.psum_scatter(contract_last(proj_bf, in_matrix).astype(jnp.bfloat16),...  354 us
    reduce_scatter x5, waiting for transfers between devices, body(): lax.psum_scatter(jnp.dot(hidden, down_matrix, preferred_element_type=jnp....  341 us
    all_gather x4, blocking collectives, body(): lax.all_gather(arrived_grad.astype(jnp.bfloat16), 'wa', axis=0, tiled=True)  73 us
    psum x1, waiting for transfers between devices, body(): lax.psum(in_total.astype(jnp.bfloat16), 'seq').astype(jnp.float32)  65.1 us
  transfers between devices with their start and end apart: 99, of which 97 were waited for; matrix products, arithmetic and copies ran while one was open for 2% of the time, Pallas kernels for 0%

profile of v1, /device:TPU:1, one launch (start us, length us, event | category | flops | bytes accessed | tf_op | source)
XLA Modules:
  0.0 2372.5 jit_solution(10258096485236485752)
XLA Ops:
  15.6 88.3 %all-reduce.14.cloned.1.call-done = f32[256,1024]{1,0:T(8,128)} async-done(((f32[256,1024]{1,0:T(8,128)}), f32[256,1024]{1,0:T(8,128)}) %all-reduce.14.cloned.1.call-update) | async-done | bytes 1048592 | tf_op jit(solution)/shard_map/psum | solution.py:97
  108.8 72.1 %reduce-scatter.11.cloned.1.call-done = f32[16,1024]{1,0:T(8,128)} async-done(((f32[256,1024]{1,0:T(8,128)}), f32[16,1024]{1,0:T(8,128)}) %reduce-scatter.11.cloned.1.call-update) | async-done | bytes 65552 | tf_op jit(solution)/shard_map/reduce_scatter | solution.py:112
  222.5 6.4 collective-permute-done.8
  259.4 6.1 collective-permute-done.14
  286.6 98.5 %all-reduce.16.cloned.1.call-done = f32[256,1024]{1,0:T(8,128)} async-done(((f32[256,1024]{1,0:T(8,128)}), f32[256,1024]{1,0:T(8,128)}) %all-reduce.16.cloned.1.call-update) | async-done | bytes 1048592 | tf_op jit(solution)/shard_map/psum | solution.py:97
  390.1 72.2 %reduce-scatter.13.cloned.1.call-done = f32[16,1024]{1,0:T(8,128)} async-done(((f32[256,1024]{1,0:T(8,128)}), f32[16,1024]{1,0:T(8,128)}) %reduce-scatter.13.cloned.1.call-update) | async-done | bytes 65552 | tf_op jit(solution)/shard_map/reduce_scatter | solution.py:112
  504.0 6.4 collective-permute-done.25
  540.9 6.1 collective-permute-done.31
  574.2 98.3 %all-reduce.18.cloned.1.call-done = f32[256,1024]{1,0:T(8,128)} async-done(((f32[256,1024]{1,0:T(8,128)}), f32[256,1024]{1,0:T(8,128)}) %all-reduce.18.cloned.1.call-update) | async-done | bytes 1048592 | tf_op jit(solution)/shard_map/psum | solution.py:97
  677.7 72.1 %reduce-scatter.15.cloned.1.call-done = f32[16,1024]{1,0:T(8,128)} async-done(((f32[256,1024]{1,0:T(8,128)}), f32[16,1024]{1,0:T(8,128)}) %reduce-scatter.15.cloned.1.call-update) | async-done | bytes 65552 | tf_op jit(solution)/shard_map/reduce_scatter | solution.py:112
  791.4 6.4 collective-permute-done.42
  862.1 98.3 %all-reduce.20.cloned.1.call-done = f32[256,1024]{1,0:T(8,128)} async-done(((f32[256,1024]{1,0:T(8,128)}), f32[256,1024]{1,0:T(8,128)}) %all-reduce.20.cloned.1.call-update) | async-done | bytes 1048592 | tf_op jit(solution)/shard_map/psum | solution.py:97
  965.6 72.1 %reduce-scatter.17.cloned.1.call-done = f32[16,1024]{1,0:T(8,128)} async-done(((f32[256,1024]{1,0:T(8,128)}), f32[16,1024]{1,0:T(8,128)}) %reduce-scatter.17.cloned.1.call-update) | async-done | bytes 65552 | tf_op jit(solution)/shard_map/reduce_scatter | solution.py:112
  1079.4 6.4 collective-permute-done.59
  1149.7 98.1 %all-reduce.22.cloned.1.call-done = f32[256,1024]{1,0:T(8,128)} async-done(((f32[256,1024]{1,0:T(8,128)}), f32[256,1024]{1,0:T(8,128)}) %all-reduce.22.cloned.1.call-update) | async-done | bytes 1048592 | tf_op jit(solution)/shard_map/psum | solution.py:97
  1255.7 84.7 %all-reduce.24.cloned.1.call-done = bf16[256,1024]{1,0:T(8,128)(2,1)} async-done(((bf16[256,1024]{1,0:T(8,128)(2,1)}), bf16[256,1024]{1,0:T(8,128)(2,1)}) %all-reduce.24.cloned.1.call-update) | async-done | bytes 524304 | tf_op jit(solution)/shard_map/psum | solution.py:177
  1351.0 72.9 %reduce-scatter.21.cloned.1.call-done = bf16[16,1024]{1,0:T(8,128)(2,1)} async-done(((bf16[256,1024]{1,0:T(8,128)(2,1)}), bf16[16,1024]{1,0:T(8,128)(2,1)}) %reduce-scatter.21.cloned.1.call-update) | async-done | bytes 32784 | tf_op jit(solution)/shard_map/reduce_scatter | solution.py:213
  1430.4 18.2 all_gather.12
  1452.9 87.5 %all-reduce.26.cloned.1.call-done = bf16[256,1024]{1,0:T(8,128)(2,1)} async-done(((bf16[256,1024]{1,0:T(8,128)(2,1)}), bf16[256,1024]{1,0:T(8,128)(2,1)}) %all-reduce.26.cloned.1.call-update) | async-done | bytes 524304 | tf_op jit(solution)/shard_map/psum | solution.py:177
  1551.1 72.9 %reduce-scatter.23.cloned.1.call-done = bf16[16,1024]{1,0:T(8,128)(2,1)} async-done(((bf16[256,1024]{1,0:T(8,128)(2,1)}), bf16[16,1024]{1,0:T(8,128)(2,1)}) %reduce-scatter.23.cloned.1.call-update) | async-done | bytes 32784 | tf_op jit(solution)/shard_map/reduce_scatter | solution.py:213
  1630.6 18.1 all_gather.13
  1653.1 87.5 %all-reduce.28.cloned.1.call-done = bf16[256,1024]{1,0:T(8,128)(2,1)} async-done(((bf16[256,1024]{1,0:T(8,128)(2,1)}), bf16[256,1024]{1,0:T(8,128)(2,1)}) %all-reduce.28.cloned.1.call-update) | async-done | bytes 524304 | tf_op jit(solution)/shard_map/psum | solution.py:177
  1751.3 72.9 %reduce-scatter.25.cloned.1.call-done = bf16[16,1024]{1,0:T(8,128)(2,1)} async-done(((bf16[256,1024]{1,0:T(8,128)(2,1)}), bf16[16,1024]{1,0:T(8,128)(2,1)}) %reduce-scatter.25.cloned.1.call-update) | async-done | bytes 32784 | tf_op jit(solution)/shard_map/reduce_scatter | solution.py:213
  1830.7 18.1 all_gather.14
  1853.4 87.3 %all-reduce.30.cloned.1.call-done = bf16[256,1024]{1,0:T(8,128)(2,1)} async-done(((bf16[256,1024]{1,0:T(8,128)(2,1)}), bf16[256,1024]{1,0:T(8,128)(2,1)}) %all-reduce.30.cloned.1.call-update) | async-done | bytes 524304 | tf_op jit(solution)/shard_map/psum | solution.py:177
  1952.1 71.8 %reduce-scatter.27.cloned.1.call-done = bf16[16,1024]{1,0:T(8,128)(2,1)} async-done(((bf16[256,1024]{1,0:T(8,128)(2,1)}), bf16[16,1024]{1,0:T(8,128)(2,1)}) %reduce-scatter.27.cloned.1.call-update) | async-done | bytes 32784 | tf_op jit(solution)/shard_map/reduce_scatter | solution.py:213
  2032.2 18.6 all_gather.15
  2078.3 63.0 %all-reduce.32.cloned.1.call-done = bf16[256,1024]{1,0:T(8,128)(2,1)} async-done(((bf16[256,1024]{1,0:T(8,128)(2,1)}), bf16[256,1024]{1,0:T(8,128)(2,1)}) %all-reduce.32.cloned.1.call-update) | async-done | bytes 524304 | tf_op jit(solution)/shard_map/psum | solution.py:177
  2164.3 52.6 %reduce-scatter.19.cloned.1.call-done = f32[16,1024]{1,0:T(8,128)} async-done(((f32[256,1024]{1,0:T(8,128)}), f32[16,1024]{1,0:T(8,128)}) %reduce-scatter.19.cloned.1.call-update) | async-done | bytes 65552 | tf_op jit(solution)/shard_map/reduce_scatter | solution.py:112
  2218.7 8.5 all-reduce
  2228.4 63.1 %reduce-scatter.29.cloned.1.call-done = bf16[16,1024]{1,0:T(8,128)(2,1)} async-done(((bf16[256,1024]{1,0:T(8,128)(2,1)}), bf16[16,1024]{1,0:T(8,128)(2,1)}) %reduce-scatter.29.cloned.1.call-update) | async-done | bytes 32784 | tf_op jit(solution)/shard_map/reduce_scatter | solution.py:213
  2293.0 65.1 %all-reduce.34.cloned.1.call-done = (bf16[1,1024,3,64]{1,3,2,0:T(8,128)(2,1)}, bf16[1,64,1024]{2,1,0:T(8,128)(2,1)}, bf16[1,1024,2,288]{1,3,2,0:T(8,128)(2,1)}, bf16[1,288,1024]{2,1,0:T(8,128)(2,1)}) async-done(((bf16[1,1024,3,64]{1,3,2,0:T(8,128)(2,1)}, bf16[1,64,1024]{2,1,0:T(8,128)(2,1)}, bf16[1,1024,2,288]{1,3,2,0:T(8,128)(2,1)}, bf16[1,288,1024]{2,1,0:T(8,128)(2,1)}), ...) | async-done | bytes 2293776 | tf_op jit(solution)/shard_map/psum | solution.py:236
  (776 shorter events, 584.3 us)
Async XLA Ops:
  7.2 96.8 %all-reduce.14.cloned.1.call-start = ((), (), s32[]{:S(2)}) async-start(), calls=%async_computation.10 | async-start | bytes 2097152 | tf_op jit(solution)/shard_map/psum | solution.py:97
  15.6 165.3 %reduce-scatter.11.cloned.1.call-start = ((), (), s32[]{:S(2)}) async-start(), calls=%async_computation.11 | async-start | bytes 1114112 | tf_op jit(solution)/shard_map/reduce_scatter | solution.py:112
  108.8 276.3 %all-reduce.16.cloned.1.call-start = ((), (), s32[]{:S(2)}) async-start(), calls=%async_computation.12 | async-start | bytes 2097152 | tf_op jit(solution)/shard_map/psum | solution.py:97
  222.5 6.4 collective-permute-start.8
  229.0 6.1 collective-permute-start.9
  259.4 6.1 collective-permute-start.14
  286.6 175.7 %reduce-scatter.13.cloned.1.call-start = ((), (), s32[]{:S(2)}) async-start(), calls=%async_computation.13 | async-start | bytes 1114112 | tf_op jit(solution)/shard_map/reduce_scatter | solution.py:112
  390.0 282.5 %all-reduce.18.cloned.1.call-start = ((), (), s32[]{:S(2)}) async-start(), calls=%async_computation.14 | async-start | bytes 2097152 | tf_op jit(solution)/shard_map/psum | solution.py:97
  479.5 6.3 collective-permute-start.21
  504.0 6.4 collective-permute-start.25
  540.9 6.1 collective-permute-start.31
  574.2 175.6 %reduce-scatter.15.cloned.1.call-start = ((), (), s32[]{:S(2)}) async-start(), calls=%async_computation.15 | async-start | bytes 1114112 | tf_op jit(solution)/shard_map/reduce_scatter | solution.py:112
  677.6 282.8 %all-reduce.20.cloned.1.call-start = ((), (), s32[]{:S(2)}) async-start(), calls=%async_computation.16 | async-start | bytes 2097152 | tf_op jit(solution)/shard_map/psum | solution.py:97
  791.4 6.4 collective-permute-start.42
  828.3 6.5 collective-permute-start.48
  862.0 175.7 %reduce-scatter.17.cloned.1.call-start = ((), (), s32[]{:S(2)}) async-start(), calls=%async_computation.17 | async-start | bytes 1114112 | tf_op jit(solution)/shard_map/reduce_scatter | solution.py:112
  965.6 282.3 %all-reduce.22.cloned.1.call-start = ((), (), s32[]{:S(2)}) async-start(), calls=%async_computation.18 | async-start | bytes 2097152 | tf_op jit(solution)/shard_map/psum | solution.py:97
  1079.4 6.4 collective-permute-start.59
  1116.2 6.1 collective-permute-start.65
  1149.5 190.9 %all-reduce.24.cloned.1.call-start = ((), (), s32[]{:S(2)}) async-start(), calls=%async_computation.20 | async-start | bytes 1048576 | tf_op jit(solution)/shard_map/psum | solution.py:177
  1255.7 168.2 %reduce-scatter.21.cloned.1.call-start = ((), (), s32[]{:S(2)}) async-start(), calls=%async_computation.21 | async-start | bytes 557056 | tf_op jit(solution)/shard_map/reduce_scatter | solution.py:213
  1350.9 189.5 %all-reduce.26.cloned.1.call-start = ((), (), s32[]{:S(2)}) async-start(), calls=%async_computation.22 | async-start | bytes 1048576 | tf_op jit(solution)/shard_map/psum | solution.py:177
  1452.9 171.2 %reduce-scatter.23.cloned.1.call-start = ((), (), s32[]{:S(2)}) async-start(), calls=%async_computation.23 | async-start | bytes 557056 | tf_op jit(solution)/shard_map/reduce_scatter | solution.py:213
  1551.1 189.5 %all-reduce.28.cloned.1.call-start = ((), (), s32[]{:S(2)}) async-start(), calls=%async_computation.24 | async-start | bytes 1048576 | tf_op jit(solution)/shard_map/psum | solution.py:177
  1653.0 171.2 %reduce-scatter.25.cloned.1.call-start = ((), (), s32[]{:S(2)}) async-start(), calls=%async_computation.25 | async-start | bytes 557056 | tf_op jit(solution)/shard_map/reduce_scatter | solution.py:213
  1751.3 189.5 %all-reduce.30.cloned.1.call-start = ((), (), s32[]{:S(2)}) async-start(), calls=%async_computation.26 | async-start | bytes 1048576 | tf_op jit(solution)/shard_map/psum | solution.py:177
  1853.2 170.7 %reduce-scatter.27.cloned.1.call-start = ((), (), s32[]{:S(2)}) async-start(), calls=%async_computation.27 | async-start | bytes 557056 | tf_op jit(solution)/shard_map/reduce_scatter | solution.py:213
  1950.8 190.4 %all-reduce.32.cloned.1.call-start = ((), (), s32[]{:S(2)}) async-start(), calls=%async_computation.28 | async-start | bytes 1048576 | tf_op jit(solution)/shard_map/psum | solution.py:177
  2025.3 6.9 collective-permute-start.76
  2054.8 162.1 %reduce-scatter.19.cloned.1.call-start = ((), (), s32[]{:S(2)}) async-start(), calls=%async_computation.19 | async-start | bytes 1114112 | tf_op jit(solution)/shard_map/reduce_scatter | solution.py:112
  2060.7 230.8 %reduce-scatter.29.cloned.1.call-start = ((), (), s32[]{:S(2)}) async-start(), calls=%async_computation.29 | async-start | bytes 557056 | tf_op jit(solution)/shard_map/reduce_scatter | solution.py:213
  2151.6 206.5 %all-reduce.34.cloned.1.call-start = ((), (), s32[]{:S(2)}) async-start(), calls=%async_computation.30 | async-start | bytes 4587520 | tf_op jit(solution)/shard_map/psum | solution.py:236
  (241 other events, 3359.3 us)
Sparse Core Ops, SparseCore 0:
  15.7 88.2 all-reduce.13
  108.9 71.9 reduce-scatter.10
  286.7 98.3 all-reduce.15
  390.1 72.0 reduce-scatter.12
  574.3 98.1 all-reduce.17
  677.7 71.9 reduce-scatter.14
  862.2 98.1 all-reduce.19
  965.7 72.0 reduce-scatter.16
  1149.6 98.1 all-reduce.21
  1255.8 84.5 all-reduce.23
  1351.0 72.8 reduce-scatter.20
  1453.0 87.3 all-reduce.25
  1551.2 72.8 reduce-scatter.22
  1653.2 87.3 all-reduce.27
  1751.4 72.7 reduce-scatter.24
  1853.3 87.3 all-reduce.29
  1951.0 72.8 reduce-scatter.26
  2054.9 86.3 all-reduce.31
  2144.8 72.0 reduce-scatter.18
  2219.9 71.5 reduce-scatter.28
  2294.9 63.2 all-reduce.33
